TPU v7x, 512 devices: a whole 4x8x8 slice. The times are simulated.
512 devices in a mesh: graph: 16 (over z, core), config: 32 (over y, x).
Axes of the slice: x: 4, y: 8, z: 8, core: 2. Of those that a mesh axis runs over, the one named last changes fastest.
Arguments:
- features: bfloat16 [64, 8192, 128], P('config', 'graph'), may hold values from -6 to 6
- cotangent: bfloat16 [64, 8192, 128], P(None, ('graph', 'config')), may hold values from -6 to 6
- sage_weight: bfloat16 [2, 128, 128], replicated, may hold values from -0.5 to 0.5
- attn_weight: bfloat16 [4, 128, 128], replicated, may hold values from -0.5 to 0.5
- tile_vals: bfloat16 [192, 128, 128], P('graph'), may hold values from -0.375 to 0.375
- tile_dst: int32 [192], P('graph'), may hold values from 0 to 3
- tile_src: int32 [192], P('graph'), may hold values from 0 to 3
- tile_count: int32 [16], P('graph'), may hold values from 3 to 12, as said below
- hub_ids: int32 [128], P('graph'), may hold values from 0 to 8191, as said below
- hub_weight: bfloat16 [8192, 128], P('graph'), may hold values from -0.5 to 0.5
Outputs:
- layer_out: bfloat16 [64, 8192, 128], P(None, ('graph', 'config'))
- grad_features: bfloat16 [64, 8192, 128], P('config', 'graph')
- grad_weights: float32 [16, 6, 128, 128], P('graph')
Inputs may be any that keep to these rules, and one draw needn't show every extreme that they name: Slot t of slab g (t counted within the slab) is live when t < tile_count[g]; some slab has all 12 slots live. `hub_ids`: entries g * 8 to (g+1) * 8 - 1 are distinct nodes of slab g.
All inputs are finite; a program needn't handle non-finite values.
Results may differ from a plain program's by a relative error of at most 0.024.
Values may be sent and summed in bfloat16 or wider, within the bound.
A program may use at most 64 MiB of HBM per device.

v0:
```python
import math
import jax
import jax.numpy as jnp
from jax import lax
from jax.sharding import PartitionSpec as P

HEADS = 4
CAP = 20.0


def attend(queries, key_rows, value_rows):
    layout_count, node_count, feature_width = queries.shape
    head_size = feature_width // HEADS
    split = (layout_count, node_count, HEADS, head_size)
    query_b = queries.reshape(split)
    key_b = key_rows.reshape(split)
    value_b = value_rows.reshape(split)
    scores = jnp.einsum(
        "lkhd,mkhd->khlm", query_b, key_b, preferred_element_type=jnp.float32
    ) / math.sqrt(head_size)
    capped = CAP * jnp.tanh(scores / CAP)
    weights = jnp.exp(capped)
    attention = weights / jnp.sum(weights, axis=-1, keepdims=True)
    attention = attention.astype(value_b.dtype)
    mixture = jnp.einsum("khlm,mkhd->lkhd", attention, value_b, preferred_element_type=jnp.float32)
    return mixture.reshape(layout_count, node_count, feature_width).astype(queries.dtype)


def project(flat_rows, weight):
    return jnp.dot(flat_rows, weight, preferred_element_type=jnp.float32)


def project_back(flat_rows, weight):
    return jnp.dot(flat_rows, weight.T, preferred_element_type=jnp.float32)


def outer_sum(left_rows, right_rows):
    return jnp.dot(left_rows.T, right_rows, preferred_element_type=jnp.float32)


def sage_forward(feats, aggregate, sage_weight):
    shaped = feats.shape
    width_f = shaped[-1]
    pre_acts = project(feats.reshape(-1, width_f), sage_weight[0]) + project(
        aggregate.reshape(-1, width_f), sage_weight[1]
    )
    hidden = jax.nn.silu(pre_acts).astype(jnp.bfloat16)
    return (pre_acts.reshape(shaped), hidden.reshape(shaped))


def node_forward(hidden, attn_weight):
    shaped = hidden.shape
    width_f = shaped[-1]
    three = (shaped[0], -1, width_f)
    flat_hidden = hidden.reshape(-1, width_f)
    queries = project(flat_hidden, attn_weight[0]).astype(jnp.bfloat16)
    key_rows = project(flat_hidden, attn_weight[1]).astype(jnp.bfloat16)
    value_rows = project(flat_hidden, attn_weight[2]).astype(jnp.bfloat16)
    mixture = attend(queries.reshape(three), key_rows.reshape(three), value_rows.reshape(three))
    output = (
        flat_hidden.astype(jnp.float32) + project(mixture.reshape(-1, width_f), attn_weight[3])
    ).astype(jnp.bfloat16)
    return (
        output.reshape(shaped),
        queries.reshape(shaped),
        key_rows.reshape(shaped),
        value_rows.reshape(shaped),
        mixture.reshape(shaped),
    )


def node_backward(cot_rows, hidden, queries, key_rows, value_rows, mixture, attn_weight):
    shaped = hidden.shape
    width_f = shaped[-1]
    three = (shaped[0], -1, width_f)
    flat_cot = cot_rows.reshape(-1, width_f)
    grad_mix = project_back(flat_cot, attn_weight[3]).astype(jnp.bfloat16)
    grad_wo = outer_sum(mixture.reshape(-1, width_f), flat_cot)
    unused, pullback = jax.vjp(attend, queries, key_rows, value_rows)
    grad_q, grad_k, grad_v = pullback(grad_mix.reshape(three))
    flat_q = grad_q.reshape(-1, width_f)
    flat_k = grad_k.reshape(-1, width_f)
    flat_v = grad_v.reshape(-1, width_f)
    grad_hidden = (
        flat_cot.astype(jnp.float32)
        + project_back(flat_q, attn_weight[0])
        + project_back(flat_k, attn_weight[1])
        + project_back(flat_v, attn_weight[2])
    ).astype(jnp.bfloat16)
    flat_hidden = hidden.reshape(-1, width_f)
    grads = jnp.stack(
        [
            outer_sum(flat_hidden, flat_q),
            outer_sum(flat_hidden, flat_k),
            outer_sum(flat_hidden, flat_v),
            grad_wo,
        ]
    )
    return (grad_hidden.reshape(shaped), grads)


def sage_backward(grad_hidden, pre_acts, feats, aggregate, sage_weight):
    shaped = feats.shape
    width_f = shaped[-1]
    flat_pre = pre_acts.reshape(-1, width_f)
    sigmoid_pre = jax.nn.sigmoid(flat_pre)
    grad_pre = (
        grad_hidden.reshape(-1, width_f).astype(jnp.float32)
        * sigmoid_pre
        * (1.0 + flat_pre * (1.0 - sigmoid_pre))
    ).astype(jnp.bfloat16)
    grads = jnp.stack(
        [
            outer_sum(feats.reshape(-1, width_f), grad_pre),
            outer_sum(aggregate.reshape(-1, width_f), grad_pre),
        ]
    )
    grad_self = project_back(grad_pre, sage_weight[0]).astype(jnp.bfloat16).reshape(shaped)
    grad_agg = project_back(grad_pre, sage_weight[1]).astype(jnp.bfloat16).reshape(shaped)
    return (grad_self, grad_agg, grads)


def tile_forward(source, tile_vals, tile_src, tile_dst, live):
    layout_count, node_count, width_f = source.shape
    tile_size = tile_vals.shape[1]
    block_count = node_count // tile_size
    blocks = source.reshape(layout_count, block_count, tile_size, width_f)[:, tile_src]
    products = jnp.einsum("tij,ltjf->tlif", tile_vals, blocks, preferred_element_type=jnp.float32)
    products = products * live[:, None, None, None]
    summed = jax.ops.segment_sum(products, tile_dst, num_segments=block_count)
    return summed.transpose(1, 0, 2, 3).reshape(layout_count, node_count, width_f)


def tile_backward(grad_agg, tile_vals, tile_dst, tile_src, live):
    layout_count, node_count, width_f = grad_agg.shape
    tile_size = tile_vals.shape[1]
    block_count = node_count // tile_size
    blocks = grad_agg.reshape(layout_count, block_count, tile_size, width_f)[:, tile_dst]
    products = jnp.einsum("tij,ltif->tljf", tile_vals, blocks, preferred_element_type=jnp.float32)
    products = products * live[:, None, None, None]
    summed = jax.ops.segment_sum(products, tile_src, num_segments=block_count)
    return summed.transpose(1, 0, 2, 3).reshape(layout_count, node_count, width_f)


def flatten_nodes(arrays):
    return tuple((item.reshape(item.shape[0], -1, item.shape[-1]) for item in arrays))


def local(
    features,
    cotangent,
    sage_weight,
    attn_weight,
    tile_vals,
    tile_dst,
    tile_src,
    tile_count,
    hub_ids,
    hub_weight,
):
    layout_dev, node_dev, width_f = features.shape
    config_count = lax.axis_size("config")
    node_share = node_dev // config_count
    slab_index = lax.axis_index("graph")
    hub_local = hub_ids - slab_index * node_dev
    live = (jnp.arange(tile_dst.shape[0], dtype=jnp.int32) < tile_count[0]).astype(jnp.float32)
    local_hubs = features[:, hub_local]
    columns = hub_weight
    hub_sum = jnp.einsum(
        "nj,ljf->lnf",
        columns,
        lax.all_gather(local_hubs, "graph", axis=1, tiled=True),
        preferred_element_type=jnp.float32,
    )
    aggregate = (tile_forward(features, tile_vals, tile_src, tile_dst, live) + hub_sum).astype(
        jnp.bfloat16
    )
    split_shape = (layout_dev, config_count, node_share, width_f)
    back_shape = (layout_dev * config_count, 1, node_share, width_f)
    received = (
        lax.all_to_all(
            features.reshape(split_shape), "config", split_axis=1, concat_axis=0, tiled=True
        ),
        lax.all_to_all(
            aggregate.reshape(split_shape), "config", split_axis=1, concat_axis=0, tiled=True
        ),
    )
    pre_in, hidden_in = sage_forward(received[0], received[1], sage_weight)
    results = (received[0], received[1], pre_in, hidden_in) + node_forward(hidden_in, attn_weight)
    feats_node, agg_node, pre_node, hidden_node, output, queries, key_rows, value_rows, mixture = (
        flatten_nodes(results)
    )
    grad_hidden, attn_grads = node_backward(
        cotangent, hidden_node, queries, key_rows, value_rows, mixture, attn_weight
    )
    self_node, aggr_node, sage_grads = sage_backward(
        grad_hidden, pre_node, feats_node, agg_node, sage_weight
    )
    self_back, agg_back = (
        lax.all_to_all(
            self_node.reshape(back_shape), "config", split_axis=0, concat_axis=1, tiled=True
        ),
        lax.all_to_all(
            aggr_node.reshape(back_shape), "config", split_axis=0, concat_axis=1, tiled=True
        ),
    )
    grad_self = self_back.reshape(layout_dev, node_dev, width_f)
    grad_agg = agg_back.reshape(layout_dev, node_dev, width_f)
    back_rows = tile_backward(grad_agg, tile_vals, tile_dst, tile_src, live)
    columns = hub_weight
    hub_grads = lax.psum_scatter(
        jnp.einsum("nj,lnf->jlf", columns, grad_agg, preferred_element_type=jnp.float32).astype(
            jnp.bfloat16
        ),
        "graph",
        scatter_dimension=0,
        tiled=True,
    ).astype(jnp.float32)
    totals = grad_self.astype(jnp.float32) + back_rows
    totals = totals.at[:, hub_local].add(jnp.transpose(hub_grads, (1, 0, 2)))
    grad_features = totals.astype(jnp.bfloat16)
    partial_grads = jnp.concatenate([sage_grads, attn_grads], axis=0)
    summed = lax.psum(partial_grads.astype(jnp.bfloat16), "config").astype(jnp.float32)
    scale = 1.0 / math.sqrt(layout_dev * config_count * node_dev)
    return (output, grad_features, (summed * scale)[None])


def solution(mesh):
    return jax.shard_map(
        local,
        mesh=mesh,
        in_specs=(
            P("config", "graph", None),
            P(None, ("graph", "config"), None),
            P(),
            P(),
            P("graph", None, None),
            P("graph"),
            P("graph"),
            P("graph"),
            P("graph"),
            P("graph", None),
        ),
        out_specs=(
            P(None, ("graph", "config"), None),
            P("config", "graph", None),
            P("graph", None, None, None),
        ),
        check_vma=False,
    )
```

profile of v0, /device:TPU:1, one launch (start us, length us, event | category | flops | bytes accessed | tf_op | source)
XLA Modules:
  0.0 400.2 jit_solution(9092489679401032103)
XLA Ops:
  8.0 1.7 copy.116
  9.7 10.5 %all-to-all-start = ((bf16[2,32,16,128]{3,2,0,1:T(8,128)(2,1)}), bf16[2,32,16,128]{3,2,0,1:T(8,128)(2,1)S(1)}, u32[]{:S(2)}, u32[]{:S(2)}) async-start(bf16[2,32,16,128]{3,2,0,1:T(8,128)(2,1)} %copy.116), calls=%async_computation | async-start | bytes 524288 | tf_op jit(solution)/shard_map/all_to_all | solution.py:181
  21.6 1.5 gather_fusion.1
  24.4 1.6 gather_fusion
  26.1 1.6 multiply_bitcast_fusion.1
  27.7 1.9 copy.118
  29.6 1.8 scatter_fusion
  32.0 24.1 %all-gather = bf16[2,128,128]{2,1,0:T(8,128)(2,1)S(1)} all-gather(bf16[2,8,128]{2,1,0:T(8,128)(2,1)S(1)} %bitcast.206), channel_id=2, replica_groups=mesh['graph'=16,'config'=32] {'graph'}, dimensions={1}, use_global_device_ids=true | all-gather | bytes 69632 | tf_op jit(solution)/shard_map/all_gather | solution.py:172
  57.2 9.8 %all-to-all-start.1 = ((bf16[2,32,16,128]{3,2,0,1:T(8,128)(2,1)}), bf16[2,32,16,128]{3,2,0,1:T(8,128)(2,1)S(1)}, u32[]{:S(2)}, u32[]{:S(2)}) async-start(bf16[2,32,16,128]{3,2,0,1:T(8,128)(2,1)} %copy.121), calls=%async_computation.1 | async-start | bytes 524288 | tf_op jit(solution)/shard_map/all_to_all | solution.py:184
  68.9 1.3 dynamic-slice
  71.1 7.6 %all-to-all-done.1 = bf16[2,32,16,128]{3,2,0,1:T(8,128)(2,1)S(1)} async-done(((bf16[2,32,16,128]{3,2,0,1:T(8,128)(2,1)}), bf16[2,32,16,128]{3,2,0,1:T(8,128)(2,1)S(1)}, u32[]{:S(2)}, u32[]{:S(2)}) %all-to-all-start.1) | async-done | bytes 262176 | tf_op jit(solution)/shard_map/all_to_all | solution.py:184
  82.7 2.1 reshape_reshape.25
  84.8 1.8 copy.123
  86.6 3.2 fusion.7
  91.5 1.9 copy.124
  93.4 2.8 fusion.6
  97.2 1.5 fusion.9
  99.9 1.5 fusion.10
  101.8 1.6 copy.134
  104.0 2.5 copy.131
  108.1 2.5 copy.137
  113.1 1.5 fusion.18
  117.0 4.4 %all-to-all-start.3 = ((bf16[64,1,16,128]{3,2,1,0:T(8,128)(2,1)}), bf16[64,1,16,128]{3,2,1,0:T(8,128)(2,1)S(1)}, u32[]{:S(2)}, u32[]{:S(2)}) async-start(bf16[64,1,16,128]{3,2,1,0:T(8,128)(2,1)} %bitcast.37), calls=%async_computation.3 | async-start | bytes 524288 | tf_op jit(solution)/shard_map/all_to_all | solution.py:203
  122.6 1.6 copy.126
  124.7 1.7 fusion.13
  127.3 4.5 %all-to-all-done.3 = bf16[64,1,16,128]{3,2,1,0:T(8,128)(2,1)S(1)} async-done(((bf16[64,1,16,128]{3,2,1,0:T(8,128)(2,1)}), bf16[64,1,16,128]{3,2,1,0:T(8,128)(2,1)S(1)}, u32[]{:S(2)}, u32[]{:S(2)}) %all-to-all-start.3) | async-done | bytes 262176 | tf_op jit(solution)/shard_map/all_to_all | solution.py:203
  131.8 5.2 %all-to-all-start.2 = ((bf16[64,1,16,128]{3,2,1,0:T(8,128)(2,1)}), bf16[64,1,16,128]{3,2,1,0:T(8,128)(2,1)S(1)}, u32[]{:S(2)}, u32[]{:S(2)}) async-start(bf16[64,1,16,128]{3,2,1,0:T(8,128)(2,1)} %bitcast.32), calls=%async_computation.2 | async-start | bytes 524288 | tf_op jit(solution)/shard_map/all_to_all | solution.py:200
  137.1 136.0 %all-reduce.4.cloned.1.call-done = bf16[6,128,128]{1,2,0:T(8,128)(2,1)} async-done(((bf16[6,128,128]{1,2,0:T(8,128)(2,1)}), bf16[6,128,128]{1,2,0:T(8,128)(2,1)}) %all-reduce.4.cloned.1.call-update) | async-done | bytes 196624 | tf_op jit(solution)/shard_map/psum | solution.py:223
  275.7 1.6 multiply_bitcast_fusion
  277.3 1.9 copy.143
  279.3 1.8 scatter_fusion.1
  283.9 106.4 %all-reduce.6.cloned.1.call-done = bf16[128,2,128]{2,1,0:T(2,128)(2,1)} async-done(((bf16[128,2,128]{2,1,0:T(2,128)(2,1)}), bf16[128,2,128]{2,1,0:T(2,128)(2,1)}) %all-reduce.6.cloned.1.call-update) | async-done | bytes 65552
  (100 shorter events, 31.2 us)
Async XLA Ops:
  8.0 18.1 %copy-start = (bf16[12,128,128]{2,1,0:T(8,128)(2,1)S(1)}, bf16[12,128,128]{2,1,0:T(8,128)(2,1)}, u32[]{:S(2)}) copy-start(bf16[12,128,128]{2,1,0:T(8,128)(2,1)} %param.14) | copy-start | bytes 1179652
  9.7 47.5 %all-to-all-start = ((bf16[2,32,16,128]{3,2,0,1:T(8,128)(2,1)}), bf16[2,32,16,128]{3,2,0,1:T(8,128)(2,1)S(1)}, u32[]{:S(2)}, u32[]{:S(2)}) async-start(bf16[2,32,16,128]{3,2,0,1:T(8,128)(2,1)} %copy.116), calls=%async_computation | async-start | bytes 524288 | tf_op jit(solution)/shard_map/all_to_all | solution.py:181
  27.7 1.9 copy-start.17
  31.5 24.6 %copy-start.9 = (bf16[512,128]{1,0:T(8,128)(2,1)S(1)}, bf16[512,128]{1,0:T(8,128)(2,1)}, u32[]{:S(2)}) copy-start(bf16[512,128]{1,0:T(8,128)(2,1)} %param.19) | copy-start | bytes 393220
  31.7 35.3 %copy-start.1 = (bf16[64,16,128]{2,1,0:T(8,128)(2,1)S(1)}, bf16[64,16,128]{2,1,0:T(8,128)(2,1)}, u32[]{:S(2)}) copy-start(bf16[64,16,128]{2,1,0:T(8,128)(2,1)} %param.11) | copy-start | bytes 786436
  31.7 35.3 %copy-start.10 = (bf16[4,128,128]{2,1,0:T(8,128)(2,1)S(1)}, bf16[4,128,128]{2,1,0:T(8,128)(2,1)}, u32[]{:S(2)}) copy-start(bf16[4,128,128]{2,1,0:T(8,128)(2,1)} %param.13) | copy-start | bytes 393220
  57.2 13.6 %copy-start.13 = (bf16[2,128,128]{2,1,0:T(8,128)(2,1)S(1)}, bf16[2,128,128]{2,1,0:T(8,128)(2,1)}, u32[]{:S(2)}) copy-start(bf16[2,128,128]{2,1,0:T(8,128)(2,1)} %param.12) | copy-start | bytes 196612
  57.2 21.5 %all-to-all-start.1 = ((bf16[2,32,16,128]{3,2,0,1:T(8,128)(2,1)}), bf16[2,32,16,128]{3,2,0,1:T(8,128)(2,1)S(1)}, u32[]{:S(2)}, u32[]{:S(2)}) async-start(bf16[2,32,16,128]{3,2,0,1:T(8,128)(2,1)} %copy.121), calls=%async_computation.1 | async-start | bytes 524288 | tf_op jit(solution)/shard_map/all_to_all | solution.py:184
  78.7 2.2 copy-start.7
  89.8 0.6 copy-start.15
  93.4 2.9 copy-start.2
  93.4 2.9 copy-start.16
  97.2 1.5 copy-start.3
  98.7 2.7 copy-start.4
  99.9 1.9 copy-start.5
  103.4 3.6 copy-start.11
  113.1 1.8 copy-start.14
  113.1 2.8 copy-start.8
  114.6 2.1 copy-start.6
  117.0 14.8 %all-to-all-start.3 = ((bf16[64,1,16,128]{3,2,1,0:T(8,128)(2,1)}), bf16[64,1,16,128]{3,2,1,0:T(8,128)(2,1)S(1)}, u32[]{:S(2)}, u32[]{:S(2)}) async-start(bf16[64,1,16,128]{3,2,1,0:T(8,128)(2,1)} %bitcast.37), calls=%async_computation.3 | async-start | bytes 524288 | tf_op jit(solution)/shard_map/all_to_all | solution.py:203
  121.4 151.7 %all-reduce.4.cloned.1.call-start = ((), (), s32[]{:S(2)}) async-start(), calls=%async_computation.4 | async-start | bytes 393216 | tf_op jit(solution)/shard_map/psum | solution.py:223
  121.8 0.7 copy-start.12
  131.8 149.3 %all-to-all-start.2 = ((bf16[64,1,16,128]{3,2,1,0:T(8,128)(2,1)}), bf16[64,1,16,128]{3,2,1,0:T(8,128)(2,1)S(1)}, u32[]{:S(2)}, u32[]{:S(2)}) async-start(bf16[64,1,16,128]{3,2,1,0:T(8,128)(2,1)} %bitcast.32), calls=%async_computation.2 | async-start | bytes 524288 | tf_op jit(solution)/shard_map/all_to_all | solution.py:200
  137.0 253.3 %all-reduce.6.cloned.1.call-start = ((), (), s32[]{:S(2)}) async-start(), calls=%async_computation.5 | async-start | bytes 131072
  277.3 1.9 copy-start.18
Sparse Core Ops, SparseCore 0:
  126.0 147.0 all-reduce.3
Sparse Core Ops, SparseCore 1:
  283.4 106.9 all-reduce.5
where the time goes:
time: 401 us; the launch traced here: 400 us
  waiting for transfers between devices  255 us (64%)
  local copies, waits for them, and re-layouts  36.5 us (9%)
  starting transfers between devices  30 us (7%)
  matrix products  27.2 us (7%)
  blocking collectives  24.1 us (6%)
  between operations  17.4 us (4%)
  other arithmetic  10.5 us (3%)
    psum x1, waiting for transfers between devices, local(): lax.psum(partial_grads.astype(jnp.bfloat16), 'config').astype(jnp.float32)  136 us
    unnamed x3, waiting for transfers between devices  106 us
    all_gather x1, blocking collectives, local(): lax.all_gather(local_hubs, 'graph', axis=1, tiled=True)  24.1 us
    all_to_all x1, starting transfers between devices, local(): lax.all_to_all(features.reshape(split_shape), 'config', split_axis=1, con...  10.5 us
    all_to_all x1, starting transfers between devices, local(): lax.all_to_all(aggregate.reshape(split_shape), 'config', split_axis=1, co...  9.81 us
  transfers between devices with their start and end apart: 6, of which 4 were waited for; matrix products, arithmetic and copies ran while one was open for 7% of the time, Pallas kernels for 0%

commit v1 on v0

--- a/solution.py
+++ b/solution.py
@@ -166,12 +166,38 @@
     live = (jnp.arange(tile_dst.shape[0], dtype=jnp.int32) < tile_count[0]).astype(jnp.float32)
     local_hubs = features[:, hub_local]
     columns = hub_weight
-    hub_sum = jnp.einsum(
+    size, mine, rows = (lax.axis_size("graph"), lax.axis_index("graph"), local_hubs.shape[1])
+    right = [(i, (i + 1) % size) for i in range(size)]
+    left = [(i, (i - 1) % size) for i in range(size)]
+    middle = size // 2
+    from_left = from_right = local_hubs
+    total = jnp.einsum(
         "nj,ljf->lnf",
-        columns,
-        lax.all_gather(local_hubs, "graph", axis=1, tiled=True),
+        lax.dynamic_slice_in_dim(columns, mine * rows, local_hubs.shape[1], axis=1),
+        local_hubs,
         preferred_element_type=jnp.float32,
     )
+    for step in range(1, middle + 1):
+        from_left = lax.ppermute(from_left, "graph", right)
+        if step < size - middle:
+            from_right = lax.ppermute(from_right, "graph", left)
+            total = total + jnp.einsum(
+                "nj,ljf->lnf",
+                lax.dynamic_slice_in_dim(
+                    columns, (mine + step) % size * rows, from_right.shape[1], axis=1
+                ),
+                from_right,
+                preferred_element_type=jnp.float32,
+            )
+        total = total + jnp.einsum(
+            "nj,ljf->lnf",
+            lax.dynamic_slice_in_dim(
+                columns, (mine - step) % size * rows, from_left.shape[1], axis=1
+            ),
+            from_left,
+            preferred_element_type=jnp.float32,
+        )
+    hub_sum = total
     aggregate = (tile_forward(features, tile_vals, tile_src, tile_dst, live) + hub_sum).astype(
         jnp.bfloat16
     )

time: 401 us -> 414 us (1.032)
  starting transfers between devices: 30 us -> 55.8 us
  blocking collectives: 24.1 us -> 0 us
  waiting for transfers between devices: 255 us -> 261 us
  matrix products: 27.2 us -> 32.7 us
    ppermute x0 -> x15, starting transfers between devices: none -> 31 us  [the longest x7 30.2 us: local(): from_right = lax.ppermute(from_right, 'graph', left)]
    all_gather x1 -> x0, blocking collectives: 24.1 us -> none  [local(): lax.all_gather(local_hubs, 'graph', axis=1, tiled=True)]
    dot_general x1 -> x16, matrix products: 0.24 us -> 6.77 us  [the longest x8 2.54 us: local(): jnp.einsum('nj,ljf->lnf', lax.dynamic_slice_in_dim(columns, (mine - step)...]
  transfers between devices with their start and end apart: 6 -> 21, of which waited for: 4 -> 10; matrix products, arithmetic and copies ran while one was open for 7% -> 8% of each run, Pallas kernels for 0% -> 0%
where the time goes in v1:
time: 414 us; the launch traced here: 413 us
  waiting for transfers between devices  261 us (63%)
  starting transfers between devices  55.8 us (13%)
  local copies, waits for them, and re-layouts  35 us (8%)
  matrix products  32.7 us (8%)
  between operations  18 us (4%)
  other arithmetic  10.6 us (3%)
    psum x1, waiting for transfers between devices, local(): lax.psum(partial_grads.astype(jnp.bfloat16), 'config').astype(jnp.float32)  139 us
    unnamed x3, waiting for transfers between devices  106 us
    ppermute x7, starting transfers between devices, local(): from_right = lax.ppermute(from_right, 'graph', left)  30.2 us
    all_to_all x1, starting transfers between devices, local(): lax.all_to_all(aggregate.reshape(split_shape), 'config', split_axis=1, co...  9.73 us
  transfers between devices with their start and end apart: 21, of which 10 were waited for; matrix products, arithmetic and copies ran while one was open for 8% of the time, Pallas kernels for 0%

profile of v1, /device:TPU:1, one launch (start us, length us, event | category | flops | bytes accessed | tf_op | source)
XLA Modules:
  0.0 412.7 jit_solution(3421154221284668698)
XLA Ops:
  9.4 1.5 gather_fusion.1
  11.0 6.9 %collective-permute-start = (bf16[2,8,128]{2,1,0:T(8,128)(2,1)S(1)}, bf16[2,8,128]{2,1,0:T(8,128)(2,1)S(1)}, u32[]{:S(2)}, u32[]{:S(2)}) collective-permute-start(bf16[2,8,128]{2,1,0:T(8,128)(2,1)S(1)} %bitcast.281), channel_id=1, source_target_pairs={{0,480},{32,0},{64,32},{96,64},{128,96},{160,128},{192,160},{224,1... | collective-permute-start | bytes 12296 | tf_op jit(solution)/shard_map/ppermute | solution.py:183
  17.8 1.7 copy.164
  19.5 6.4 %all-to-all-start = ((bf16[2,32,16,128]{3,2,0,1:T(8,128)(2,1)}), bf16[2,32,16,128]{3,2,0,1:T(8,128)(2,1)}, u32[]{:S(2)}, u32[]{:S(2)}) async-start(bf16[2,32,16,128]{3,2,0,1:T(8,128)(2,1)} %copy.164), calls=%async_computation | async-start | bytes 524288 | tf_op jit(solution)/shard_map/all_to_all | solution.py:207
  27.5 2.0 fusion.66
  31.2 1.9 scatter_fusion
  34.5 6.0 %collective-permute-start.2 = (bf16[2,8,128]{2,1,0:T(8,128)(2,1)S(1)}, bf16[2,8,128]{2,1,0:T(8,128)(2,1)S(1)}, u32[]{:S(2)}, u32[]{:S(2)}) collective-permute-start(bf16[2,8,128]{2,1,0:T(8,128)(2,1)S(1)} %collective-permute-done), channel_id=1, source_target_pairs={{0,480},{32,0},{64,32},{96,64},{128,96},{160,128},{192,160},{224,1... | collective-permute-start | bytes 12296 | tf_op jit(solution)/shard_map/ppermute | solution.py:183
  41.6 3.5 collective-permute-start.4
  45.9 3.5 collective-permute-start.6
  50.2 3.4 collective-permute-start.8
  54.5 3.4 collective-permute-start.10
  58.7 3.4 collective-permute-start.12
  63.3 3.4 collective-permute-done.14
  67.9 9.7 %all-to-all-start.1 = ((bf16[2,32,16,128]{3,2,0,1:T(8,128)(2,1)}), bf16[2,32,16,128]{3,2,0,1:T(8,128)(2,1)S(1)}, u32[]{:S(2)}, u32[]{:S(2)}) async-start(bf16[2,32,16,128]{3,2,0,1:T(8,128)(2,1)} %copy.185), calls=%async_computation.1 | async-start | bytes 524288 | tf_op jit(solution)/shard_map/all_to_all | solution.py:210
  82.6 5.3 %all-to-all-done.1 = bf16[2,32,16,128]{3,2,0,1:T(8,128)(2,1)S(1)} async-done(((bf16[2,32,16,128]{3,2,0,1:T(8,128)(2,1)}), bf16[2,32,16,128]{3,2,0,1:T(8,128)(2,1)S(1)}, u32[]{:S(2)}, u32[]{:S(2)}) %all-to-all-start.1) | async-done | bytes 262176 | tf_op jit(solution)/shard_map/all_to_all | solution.py:210
  91.9 2.1 reshape_reshape.25
  94.0 1.8 copy.187
  95.8 3.2 fusion.7
  100.7 1.8 copy.188
  102.6 2.8 fusion.6
  111.0 1.6 copy.198
  113.1 2.5 copy.195
  117.2 2.5 copy.201
  127.2 3.9 all-to-all-start.3
  132.2 1.6 copy.190
  136.2 5.4 %all-to-all-done.3 = bf16[64,1,16,128]{3,2,1,0:T(8,128)(2,1)S(1)} async-done(((bf16[64,1,16,128]{3,2,1,0:T(8,128)(2,1)}), bf16[64,1,16,128]{3,2,1,0:T(8,128)(2,1)S(1)}, u32[]{:S(2)}, u32[]{:S(2)}) %all-to-all-start.3) | async-done | bytes 262176 | tf_op jit(solution)/shard_map/all_to_all | solution.py:229
  141.6 4.6 %all-to-all-start.2 = ((bf16[64,1,16,128]{3,2,1,0:T(8,128)(2,1)}), bf16[64,1,16,128]{3,2,1,0:T(8,128)(2,1)}, u32[]{:S(2)}, u32[]{:S(2)}) async-start(bf16[64,1,16,128]{3,2,1,0:T(8,128)(2,1)} %bitcast.47), calls=%async_computation.2 | async-start | bytes 524288 | tf_op jit(solution)/shard_map/all_to_all | solution.py:226
  146.3 139.3 %all-reduce.4.cloned.1.call-done = bf16[6,128,128]{1,2,0:T(8,128)(2,1)} async-done(((bf16[6,128,128]{1,2,0:T(8,128)(2,1)}), bf16[6,128,128]{1,2,0:T(8,128)(2,1)}) %all-reduce.4.cloned.1.call-update) | async-done | bytes 196624 | tf_op jit(solution)/shard_map/psum | solution.py:249
  288.2 1.6 multiply_bitcast_fusion
  289.8 1.9 copy.207
  291.8 1.8 scatter_fusion.1
  296.5 106.4 %all-reduce.6.cloned.1.call-done = bf16[128,2,128]{2,1,0:T(2,128)(2,1)} async-done(((bf16[128,2,128]{2,1,0:T(2,128)(2,1)}), bf16[128,2,128]{2,1,0:T(2,128)(2,1)}) %all-reduce.6.cloned.1.call-update) | async-done | bytes 65552
  (152 shorter events, 47.5 us)
Async XLA Ops:
  8.0 22.2 %copy-start = (bf16[12,128,128]{2,1,0:T(8,128)(2,1)S(1)}, bf16[12,128,128]{2,1,0:T(8,128)(2,1)}, u32[]{:S(2)}) copy-start(bf16[12,128,128]{2,1,0:T(8,128)(2,1)} %param.14) | copy-start | bytes 1179652
  8.0 21.5 %copy-start.2 = (bf16[2,512,128]{2,1,0:T(8,128)(2,1)S(1)}, bf16[2,512,128]{2,1,0:T(8,128)(2,1)}, u32[]{:S(2)}) copy-start(bf16[2,512,128]{2,1,0:T(8,128)(2,1)} %param.10) | copy-start | bytes 786436
  9.4 20.1 %copy-start.20 = (s32[8]{0:T(128)}, s32[8]{0:T(128)S(1)}, u32[]{:S(2)}) copy-start(s32[8]{0:T(128)S(1)} %compare_select_fusion.1) | copy-start | bytes 100
  11.0 23.6 %collective-permute-start = (bf16[2,8,128]{2,1,0:T(8,128)(2,1)S(1)}, bf16[2,8,128]{2,1,0:T(8,128)(2,1)S(1)}, u32[]{:S(2)}, u32[]{:S(2)}) collective-permute-start(bf16[2,8,128]{2,1,0:T(8,128)(2,1)S(1)} %bitcast.281), channel_id=1, source_target_pairs={{0,480},{32,0},{64,32},{96,64},{128,96},{160,128},{192,160},{224,1... | collective-permute-start | bytes 12296 | tf_op jit(solution)/shard_map/ppermute | solution.py:183
  17.8 15.9 %collective-permute-start.1 = (bf16[2,8,128]{2,1,0:T(8,128)(2,1)S(1)}, bf16[2,8,128]{2,1,0:T(8,128)(2,1)S(1)}, u32[]{:S(2)}, u32[]{:S(2)}) collective-permute-start(bf16[2,8,128]{2,1,0:T(8,128)(2,1)S(1)} %bitcast.282), channel_id=1, source_target_pairs={{0,32},{32,64},{64,96},{96,128},{128,160},{160,192},{192,224},{224... | collective-permute-start | bytes 12296 | tf_op jit(solution)/shard_map/ppermute | solution.py:181
  19.5 48.4 %all-to-all-start = ((bf16[2,32,16,128]{3,2,0,1:T(8,128)(2,1)}), bf16[2,32,16,128]{3,2,0,1:T(8,128)(2,1)}, u32[]{:S(2)}, u32[]{:S(2)}) async-start(bf16[2,32,16,128]{3,2,0,1:T(8,128)(2,1)} %copy.164), calls=%async_computation | async-start | bytes 524288 | tf_op jit(solution)/shard_map/all_to_all | solution.py:207
  26.8 3.8 copy-start.18
  33.2 7.4 %copy-start.1 = (bf16[512,128]{1,0:T(8,128)(2,1)S(1)}, bf16[512,128]{1,0:T(8,128)(2,1)}, u32[]{:S(2)}) copy-start(bf16[512,128]{1,0:T(8,128)(2,1)} %param.19) | copy-start | bytes 393220
  33.2 7.4 %copy-start.5 = (f32[2,128,512]{2,1,0:T(8,128)S(1)}, f32[2,128,512]{2,1,0:T(8,128)}, u32[]{:S(2)}) copy-start(f32[2,128,512]{2,1,0:T(8,128)} %fusion.66) | copy-start | bytes 1572868
  33.8 7.5 %collective-permute-start.3 = (bf16[2,8,128]{2,1,0:T(8,128)(2,1)S(1)}, bf16[2,8,128]{2,1,0:T(8,128)(2,1)S(1)}, u32[]{:S(2)}, u32[]{:S(2)}) collective-permute-start(bf16[2,8,128]{2,1,0:T(8,128)(2,1)S(1)} %collective-permute-done.1), channel_id=1, source_target_pairs={{0,32},{32,64},{64,96},{96,128},{128,160},{160,192},{192,224},{224... | collective-permute-start | bytes 12296 | tf_op jit(solution)/shard_map/ppermute | solution.py:181
  34.5 7.0 %collective-permute-start.2 = (bf16[2,8,128]{2,1,0:T(8,128)(2,1)S(1)}, bf16[2,8,128]{2,1,0:T(8,128)(2,1)S(1)}, u32[]{:S(2)}, u32[]{:S(2)}) collective-permute-start(bf16[2,8,128]{2,1,0:T(8,128)(2,1)S(1)} %collective-permute-done), channel_id=1, source_target_pairs={{0,480},{32,0},{64,32},{96,64},{128,96},{160,128},{192,160},{224,1... | collective-permute-start | bytes 12296 | tf_op jit(solution)/shard_map/ppermute | solution.py:183
  41.2 4.2 %collective-permute-start.5 = (bf16[2,8,128]{2,1,0:T(8,128)(2,1)S(1)}, bf16[2,8,128]{2,1,0:T(8,128)(2,1)S(1)}, u32[]{:S(2)}, u32[]{:S(2)}) collective-permute-start(bf16[2,8,128]{2,1,0:T(8,128)(2,1)S(1)} %collective-permute-done.3), channel_id=1, source_target_pairs={{0,32},{32,64},{64,96},{96,128},{128,160},{160,192},{192,224},{224... | collective-permute-start | bytes 12296 | tf_op jit(solution)/shard_map/ppermute | solution.py:181
  41.6 4.3 %collective-permute-start.4 = (bf16[2,8,128]{2,1,0:T(8,128)(2,1)S(1)}, bf16[2,8,128]{2,1,0:T(8,128)(2,1)S(1)}, u32[]{:S(2)}, u32[]{:S(2)}) collective-permute-start(bf16[2,8,128]{2,1,0:T(8,128)(2,1)S(1)} %collective-permute-done.2), channel_id=1, source_target_pairs={{0,480},{32,0},{64,32},{96,64},{128,96},{160,128},{192,160},{224,1... | collective-permute-start | bytes 12296 | tf_op jit(solution)/shard_map/ppermute | solution.py:183
  45.5 4.3 %collective-permute-start.7 = (bf16[2,8,128]{2,1,0:T(8,128)(2,1)S(1)}, bf16[2,8,128]{2,1,0:T(8,128)(2,1)S(1)}, u32[]{:S(2)}, u32[]{:S(2)}) collective-permute-start(bf16[2,8,128]{2,1,0:T(8,128)(2,1)S(1)} %collective-permute-done.5), channel_id=1, source_target_pairs={{0,32},{32,64},{64,96},{96,128},{128,160},{160,192},{192,224},{224... | collective-permute-start | bytes 12296 | tf_op jit(solution)/shard_map/ppermute | solution.py:181
  45.9 4.3 %collective-permute-start.6 = (bf16[2,8,128]{2,1,0:T(8,128)(2,1)S(1)}, bf16[2,8,128]{2,1,0:T(8,128)(2,1)S(1)}, u32[]{:S(2)}, u32[]{:S(2)}) collective-permute-start(bf16[2,8,128]{2,1,0:T(8,128)(2,1)S(1)} %collective-permute-done.4), channel_id=1, source_target_pairs={{0,480},{32,0},{64,32},{96,64},{128,96},{160,128},{192,160},{224,1... | collective-permute-start | bytes 12296 | tf_op jit(solution)/shard_map/ppermute | solution.py:183
  49.7 4.2 %collective-permute-start.9 = (bf16[2,8,128]{2,1,0:T(8,128)(2,1)S(1)}, bf16[2,8,128]{2,1,0:T(8,128)(2,1)S(1)}, u32[]{:S(2)}, u32[]{:S(2)}) collective-permute-start(bf16[2,8,128]{2,1,0:T(8,128)(2,1)S(1)} %collective-permute-done.7), channel_id=1, source_target_pairs={{0,32},{32,64},{64,96},{96,128},{128,160},{160,192},{192,224},{224... | collective-permute-start | bytes 12296 | tf_op jit(solution)/shard_map/ppermute | solution.py:181
  50.2 4.2 %collective-permute-start.8 = (bf16[2,8,128]{2,1,0:T(8,128)(2,1)S(1)}, bf16[2,8,128]{2,1,0:T(8,128)(2,1)S(1)}, u32[]{:S(2)}, u32[]{:S(2)}) collective-permute-start(bf16[2,8,128]{2,1,0:T(8,128)(2,1)S(1)} %collective-permute-done.6), channel_id=1, source_target_pairs={{0,480},{32,0},{64,32},{96,64},{128,96},{160,128},{192,160},{224,1... | collective-permute-start | bytes 12296 | tf_op jit(solution)/shard_map/ppermute | solution.py:183
  54.0 4.2 %collective-permute-start.11 = (bf16[2,8,128]{2,1,0:T(8,128)(2,1)S(1)}, bf16[2,8,128]{2,1,0:T(8,128)(2,1)S(1)}, u32[]{:S(2)}, u32[]{:S(2)}) collective-permute-start(bf16[2,8,128]{2,1,0:T(8,128)(2,1)S(1)} %collective-permute-done.9), channel_id=1, source_target_pairs={{0,32},{32,64},{64,96},{96,128},{128,160},{160,192},{192,224},{224... | collective-permute-start | bytes 12296 | tf_op jit(solution)/shard_map/ppermute | solution.py:181
  54.5 4.2 %collective-permute-start.10 = (bf16[2,8,128]{2,1,0:T(8,128)(2,1)S(1)}, bf16[2,8,128]{2,1,0:T(8,128)(2,1)S(1)}, u32[]{:S(2)}, u32[]{:S(2)}) collective-permute-start(bf16[2,8,128]{2,1,0:T(8,128)(2,1)S(1)} %collective-permute-done.8), channel_id=1, source_target_pairs={{0,480},{32,0},{64,32},{96,64},{128,96},{160,128},{192,160},{224,1... | collective-permute-start | bytes 12296 | tf_op jit(solution)/shard_map/ppermute | solution.py:183
  58.2 4.2 %collective-permute-start.13 = (bf16[2,8,128]{2,1,0:T(8,128)(2,1)S(1)}, bf16[2,8,128]{2,1,0:T(8,128)(2,1)S(1)}, u32[]{:S(2)}, u32[]{:S(2)}) collective-permute-start(bf16[2,8,128]{2,1,0:T(8,128)(2,1)S(1)} %collective-permute-done.11), channel_id=1, source_target_pairs={{0,32},{32,64},{64,96},{96,128},{128,160},{160,192},{192,224},{224... | collective-permute-start | bytes 12296 | tf_op jit(solution)/shard_map/ppermute | solution.py:181
  58.7 4.2 %collective-permute-start.12 = (bf16[2,8,128]{2,1,0:T(8,128)(2,1)S(1)}, bf16[2,8,128]{2,1,0:T(8,128)(2,1)S(1)}, u32[]{:S(2)}, u32[]{:S(2)}) collective-permute-start(bf16[2,8,128]{2,1,0:T(8,128)(2,1)S(1)} %collective-permute-done.10), channel_id=1, source_target_pairs={{0,480},{32,0},{64,32},{96,64},{128,96},{160,128},{192,160},{224,1... | collective-permute-start | bytes 12296 | tf_op jit(solution)/shard_map/ppermute | solution.py:183
  62.5 4.2 %collective-permute-start.14 = (bf16[2,8,128]{2,1,0:T(8,128)(2,1)S(1)}, bf16[2,8,128]{2,1,0:T(8,128)(2,1)S(1)}, u32[]{:S(2)}, u32[]{:S(2)}) collective-permute-start(bf16[2,8,128]{2,1,0:T(8,128)(2,1)S(1)} %collective-permute-done.13), channel_id=1, source_target_pairs={{0,32},{32,64},{64,96},{96,128},{128,160},{160,192},{192,224},{224... | collective-permute-start | bytes 12296 | tf_op jit(solution)/shard_map/ppermute | solution.py:181
  62.8 14.8 %copy-start.3 = (bf16[64,16,128]{2,1,0:T(8,128)(2,1)S(1)}, bf16[64,16,128]{2,1,0:T(8,128)(2,1)}, u32[]{:S(2)}) copy-start(bf16[64,16,128]{2,1,0:T(8,128)(2,1)} %param.11) | copy-start | bytes 786436
  62.8 14.8 %copy-start.12 = (bf16[4,128,128]{2,1,0:T(8,128)(2,1)S(1)}, bf16[4,128,128]{2,1,0:T(8,128)(2,1)}, u32[]{:S(2)}) copy-start(bf16[4,128,128]{2,1,0:T(8,128)(2,1)} %param.13) | copy-start | bytes 393220
  67.9 13.5 %copy-start.14 = (bf16[2,128,128]{2,1,0:T(8,128)(2,1)S(1)}, bf16[2,128,128]{2,1,0:T(8,128)(2,1)}, u32[]{:S(2)}) copy-start(bf16[2,128,128]{2,1,0:T(8,128)(2,1)} %param.12) | copy-start | bytes 196612
  67.9 20.0 %all-to-all-start.1 = ((bf16[2,32,16,128]{3,2,0,1:T(8,128)(2,1)}), bf16[2,32,16,128]{3,2,0,1:T(8,128)(2,1)S(1)}, u32[]{:S(2)}, u32[]{:S(2)}) async-start(bf16[2,32,16,128]{3,2,0,1:T(8,128)(2,1)} %copy.185), calls=%async_computation.1 | async-start | bytes 524288 | tf_op jit(solution)/shard_map/all_to_all | solution.py:210
  127.2 14.5 %all-to-all-start.3 = ((bf16[64,1,16,128]{3,2,1,0:T(8,128)(2,1)}), bf16[64,1,16,128]{3,2,1,0:T(8,128)(2,1)S(1)}, u32[]{:S(2)}, u32[]{:S(2)}) async-start(bf16[64,1,16,128]{3,2,1,0:T(8,128)(2,1)} %bitcast.52), calls=%async_computation.3 | async-start | bytes 524288 | tf_op jit(solution)/shard_map/all_to_all | solution.py:229
  131.1 154.5 %all-reduce.4.cloned.1.call-start = ((), (), s32[]{:S(2)}) async-start(), calls=%async_computation.4 | async-start | bytes 393216 | tf_op jit(solution)/shard_map/psum | solution.py:249
  136.2 152.0 %copy-start.19 = (f32[12]{0:T(128)S(1)}, f32[12]{0:T(128)}, u32[]{:S(2)}) copy-start(f32[12]{0:T(128)} %copy-done.18) | copy-start | bytes 148
  141.6 152.0 %all-to-all-start.2 = ((bf16[64,1,16,128]{3,2,1,0:T(8,128)(2,1)}), bf16[64,1,16,128]{3,2,1,0:T(8,128)(2,1)}, u32[]{:S(2)}, u32[]{:S(2)}) async-start(bf16[64,1,16,128]{3,2,1,0:T(8,128)(2,1)} %bitcast.47), calls=%async_computation.2 | async-start | bytes 524288 | tf_op jit(solution)/shard_map/all_to_all | solution.py:226
  146.2 256.6 %all-reduce.6.cloned.1.call-start = ((), (), s32[]{:S(2)}) async-start(), calls=%async_computation.5 | async-start | bytes 131072
  293.6 110.0 %copy-start.21 = (s32[8]{0:T(128)S(1)}, s32[8]{0:T(128)}, u32[]{:S(2)}) copy-start(s32[8]{0:T(128)} %copy-done.20) | copy-start | bytes 100
  (12 other events, 26.8 us)
Sparse Core Ops, SparseCore 0:
  135.7 149.8 all-reduce.3
Sparse Core Ops, SparseCore 1:
  296.0 106.9 all-reduce.5
